TPU v7x, 32 devices: a whole 2x2x4 slice. The times are simulated.
32 devices in a mesh: groups: 2 (over x), dp: 16 (over z, y, core).
Axes of the slice: x: 2, y: 2, z: 4, core: 2. Of those that a mesh axis runs over, the one named last changes fastest.
Arguments:
- teacher_blocks: bfloat16 [24576, 2048], P(('groups', 'dp')), parts along dimension 0, may hold values from -9 to 9
- student_blocks: bfloat16 [24576, 2048], P(('groups', 'dp')), parts along dimension 0, may hold values from -9 to 9
- block_expert: int32 [192], P(('groups', 'dp')), parts along dimension 0, may hold values from 0 to 1
- block_count: int32 [32], P(('groups', 'dp')), parts along dimension 0, may hold values from 1 to 6, as said below
- gate_weight: bfloat16 [4, 2048, 384], P('groups'), parts along dimension 0, may hold values from -0.125 to 0.125
- up_weight: bfloat16 [4, 2048, 384], P('groups'), parts along dimension 0, may hold values from -0.125 to 0.125
Outputs:
- panels: float32 [1536, 768], P(('groups', 'dp')), parts along dimension 0
There are 2 independent parts, one for each index of `groups`. A program takes and returns all parts, laid end to end along the dimension named above; each array names one. Nothing has to cross between parts.
Inputs may be any that keep to these rules, and one draw needn't show every extreme that they name: `block_count`: at least one device holds 6 live block pairs in every draw.
All inputs are finite; a program needn't handle non-finite values.
Results may differ from a plain program's by a relative error of at most 0.00092.
Values may be sent and summed in bfloat16 or wider, within the bound.
No kernel may reach another device: no remote copies, remote signals or barrier semaphores. Data moves between devices by JAX's collectives and lax.ppermute only.
A program may use at most 64 MiB of HBM per device.

v0:
```python
import jax
import jax.numpy as jnp
from jax import lax
from jax.sharding import PartitionSpec as P


def accumulate_grams(teacher, student, experts, live_count, block_rows, gate_weight, up_weight):
    width = gate_weight.shape[2]
    expert_total = gate_weight.shape[0]

    def one_block(slot_index, accum):
        rows_teacher = lax.dynamic_slice_in_dim(teacher, slot_index * block_rows, block_rows, 0)
        rows_student = lax.dynamic_slice_in_dim(student, slot_index * block_rows, block_rows, 0)
        expert = lax.dynamic_index_in_dim(experts, slot_index, 0, keepdims=False)
        gate_matrix = lax.dynamic_index_in_dim(gate_weight, expert, 0, keepdims=False)
        up_matrix = lax.dynamic_index_in_dim(up_weight, expert, 0, keepdims=False)
        stacked = jnp.concatenate([rows_student, rows_teacher], 0)
        gate_out = jnp.dot(stacked, gate_matrix, preferred_element_type=jnp.float32)
        up_out = jnp.dot(stacked, up_matrix, preferred_element_type=jnp.float32)
        hidden = (jax.nn.silu(gate_out) * up_out).astype(jnp.bfloat16)
        hidden_student = hidden[:block_rows]
        hidden_teacher = hidden[block_rows:]
        gram_term = jnp.dot(
            hidden_student.T,
            jnp.concatenate([hidden_student, hidden_teacher], 1),
            preferred_element_type=jnp.float32,
        )
        current = lax.dynamic_slice_in_dim(accum, expert * width, width, 0)
        return lax.dynamic_update_slice_in_dim(accum, current + gram_term, expert * width, 0)

    empty = jnp.zeros((expert_total * width, 2 * width), jnp.float32)
    return lax.fori_loop(0, live_count, one_block, empty)


def local(teacher_blocks, student_blocks, block_expert, block_count, gate_weight, up_weight):
    block_rows = teacher_blocks.shape[0] // block_expert.shape[0]
    scaling = 1.0 / (block_rows * lax.axis_size("dp"))
    teacher, student, experts = (teacher_blocks, student_blocks, block_expert)
    live_count = block_count[0]
    accum = accumulate_grams(
        teacher, student, experts, live_count, block_rows, gate_weight, up_weight
    )
    summed = lax.psum_scatter(accum, "dp", scatter_dimension=0, tiled=True)
    return summed * scaling


def solution(mesh):
    return jax.shard_map(
        local,
        mesh=mesh,
        in_specs=(
            P(("groups", "dp"), None),
            P(("groups", "dp"), None),
            P(("groups", "dp")),
            P(("groups", "dp")),
            P("groups", None, None),
            P("groups", None, None),
        ),
        out_specs=P(("groups", "dp"), None),
        check_vma=False,
    )
```

profile of v0, /device:TPU:0, one launch (start us, length us, event | category | flops | bytes accessed | tf_op | source)
XLA Modules:
  0.0 136.0 jit_solution(276565505235046097)
XLA Ops:
  6.5 0.0 copy-start.2
  6.5 0.0 reduce-scatter.2.cloned.1.call-start
  6.5 0.2 broadcast_in_dim.3
  6.7 0.5 copy-done.2
  7.2 18.5 %while.10 = (s32[]{:T(128)}, f32[768,768]{1,0:T(8,128)S(1)}, s32[]{:T(128)}, s32[6]{0:T(128)S(1)}, bf16[768,2048]{1,0:T(8,128)(2,1)}, /*index=5*/bf16[768,2048]{...) while((s32[]{:T(128)}, f32[768,768]{1,0:T(8,128)S(1)}, ...), condition=%wide.region_1.2_spmd, body=%wide.region_0.1_spmd.sunk | while | flops 886276096 | bytes 23953772 | solution.py:32
  7.9 0.7 dynamic_slice.44
  11.3 1.3 constant_dynamic-slice_fusion.3
  12.6 0.0 copy-start.1
  12.6 2.3 %fusion.35 = f32[256,384]{1,0:T(8,128)S(1)} fusion(bf16[2,2048,384]{2,1,0:T(8,128)(2,1)} %get-tuple-element.163, s32[]{:T(128)S(6)} %select_n.23, bf16[128,2048]{1,0:T(8,128)(2,1)S(1)} %get-tuple-element.123, bf16[128,2048]{1,0:T(8,128)(2,1)S(1)} %get-tuple-element.124), kind=kOutput, calls=%fused_computation.2.clone.1 | convolution fusion | flops 404750336 | bytes 3014660 | tf_op jit(solution)/shard_map/while/body/dot_general | solution.py:18
  14.9 0.1 copy-done.1
  15.0 0.7 fusion.36
  15.7 0.4 fusion.38
  16.8 0.7 dynamic_slice.44
  20.2 1.3 constant_dynamic-slice_fusion.3
  21.5 0.0 copy-start.1
  21.5 2.3 %fusion.35 = f32[256,384]{1,0:T(8,128)S(1)} fusion(bf16[2,2048,384]{2,1,0:T(8,128)(2,1)} %get-tuple-element.163, s32[]{:T(128)S(6)} %select_n.23, bf16[128,2048]{1,0:T(8,128)(2,1)S(1)} %get-tuple-element.123, bf16[128,2048]{1,0:T(8,128)(2,1)S(1)} %get-tuple-element.124), kind=kOutput, calls=%fused_computation.2.clone.1 | convolution fusion | flops 404750336 | bytes 3014660 | tf_op jit(solution)/shard_map/while/body/dot_general | solution.py:18
  23.8 0.1 copy-done.1
  23.9 0.7 fusion.36
  24.6 0.4 fusion.38
  25.7 0.0 copy-start
  25.7 1.4 %copy-done = f32[768,768]{1,0:T(8,128)} copy-done((f32[768,768]{1,0:T(8,128)}, f32[768,768]{1,0:T(8,128)S(1)}, u32[]{:S(2)}) %copy-start) | copy-done | bytes 2359320
  27.1 0.0 reduce-scatter.2.cloned.1.call-update
  27.1 100.5 %reduce-scatter.2.cloned.1.call-done = f32[48,768]{1,0:T(8,128)} async-done(((f32[768,768]{1,0:T(8,128)}), f32[48,768]{1,0:T(8,128)}) %reduce-scatter.2.cloned.1.call-update) | async-done | bytes 147472 | tf_op jit(solution)/shard_map/reduce_scatter | solution.py:43
  127.6 1.6 %broadcast_multiply_fusion = f32[48,768]{1,0:T(8,128)} fusion(f32[48,768]{1,0:T(8,128)} %reduce-scatter.2.cloned.1.call-done), kind=kLoop, calls=%fused_computation.21 | loop fusion | flops 36864 | bytes 294912 | tf_op jit(solution)/shard_map/mul | solution.py:44
  (2 shorter events, 0.0 us)
Async XLA Ops:
  6.5 0.7 copy-start.2
  6.5 121.0 %reduce-scatter.2.cloned.1.call-start = ((), (), s32[]{:S(2)}) async-start(), calls=%async_computation.1 | async-start | bytes 2506752 | tf_op jit(solution)/shard_map/reduce_scatter | solution.py:43
  12.6 2.4 %copy-start.1 = (bf16[2,2048,384]{2,1,0:T(8,128)(2,1)S(1)}, bf16[2,2048,384]{2,1,0:T(8,128)(2,1)}, u32[]{:S(2)}) copy-start(bf16[2,2048,384]{2,1,0:T(8,128)(2,1)} %get-tuple-element.164) | copy-start | bytes 9437188 | tf_op jit(solution)/shard_map/while
  21.5 2.4 %copy-start.1 = (bf16[2,2048,384]{2,1,0:T(8,128)(2,1)S(1)}, bf16[2,2048,384]{2,1,0:T(8,128)(2,1)}, u32[]{:S(2)}) copy-start(bf16[2,2048,384]{2,1,0:T(8,128)(2,1)} %get-tuple-element.164) | copy-start | bytes 9437188 | tf_op jit(solution)/shard_map/while
  25.7 1.4 %copy-start = (f32[768,768]{1,0:T(8,128)}, f32[768,768]{1,0:T(8,128)S(1)}, u32[]{:S(2)}) copy-start(f32[768,768]{1,0:T(8,128)S(1)} %get-tuple-element.48) | copy-start | bytes 7077892
Sparse Core Ops, SparseCore 0:
  27.2 100.3 reduce-scatter.1
where the time goes:
time: 136 us
  waiting for transfers between devices  100 us (74%)
  between operations  13.4 us (10%)
  loops' own time  7.61 us (6%)
  matrix products  6.72 us (5%)
  local copies, waits for them, and re-layouts  6.18 us (5%)
  other arithmetic  1.58 us (1%)
    reduce_scatter x1, waiting for transfers between devices, local(): summed = lax.psum_scatter(accum, 'dp', scatter_dimension=0, tiled=True)  100 us
    another operation x1, loops' own time, accumulate_grams(): return lax.fori_loop(0, live_count, one_block, empty)  7.61 us
    dot_general x2, matrix products, one_block(): gate_out = jnp.dot(stacked, gate_matrix, preferred_element_type=jnp.float32)  4.57 us
  transfers between devices with their start and end apart: 1, of which 1 were waited for; matrix products, arithmetic and copies ran while one was open for 0% of the time, Pallas kernels for 0%

commit v1 on v0

v1 whole, which is shorter than its diff:
```python
import functools

import jax
import jax.numpy as jnp
from jax import lax
from jax.experimental import pallas as pl
from jax.experimental.pallas import tpu as pltpu
from jax.sharding import PartitionSpec as P

LANES = 128
TAIL = 16
TOP = 32700.0


def code_scale(exponent, mantissa):
    return (mantissa * (1.0 / 16384.0)) * jnp.exp2(exponent)


def write_codes(blocks, msg_ref):
    rows, width = blocks[0]().shape
    panels = width // LANES
    top = None
    for load in blocks:
        high = jnp.max(jnp.abs(load()), axis=0, keepdims=True)
        for c in range(panels):
            part = high[:, c * LANES : (c + 1) * LANES]
            top = part if top is None else jnp.maximum(top, part)
    exponent = jnp.clip(jnp.ceil(jnp.log2(jnp.maximum(top, 1e-30))), -100.0, 100.0)
    mantissa = jnp.ceil(top * jnp.exp2(-exponent) * 16384.0) + 1.0
    factor = TOP / code_scale(exponent, mantissa)
    for k, load in enumerate(blocks):
        for c in range(panels):
            part = load()[:, c * LANES : (c + 1) * LANES] * factor
            at = (k * panels + c) * rows
            msg_ref[at : at + rows, :] = jnp.round(part).astype(jnp.int32).astype(jnp.int16)
    line = lax.broadcasted_iota(jnp.int32, (TAIL, LANES), 0)
    tail = jnp.where(line == 0, exponent.astype(jnp.int32), mantissa.astype(jnp.int32))
    msg_ref[len(blocks) * panels * rows :, :] = tail.astype(jnp.int16)


def read_step(msg_ref):
    at = msg_ref.shape[0] - TAIL
    tail = msg_ref[at:, :].astype(jnp.int32).astype(jnp.float32)
    return code_scale(tail[0:1], tail[1:2]) * (1.0 / TOP)


def read_block(msg_ref, k, rows, panels, step):
    parts = []
    for c in range(panels):
        at = (k * panels + c) * rows
        parts.append(msg_ref[at : at + rows, :].astype(jnp.int32).astype(jnp.float32) * step)
    return jnp.concatenate(parts, axis=1)


def message_shape(count, rows, width):
    return jax.ShapeDtypeStruct((count * rows * (width // LANES) + TAIL, LANES), jnp.int16)


def block_offsets(orders):
    tables = []
    for order in orders:
        depth = len(order)
        tables.append(
            [
                sum(bit for i, bit in enumerate(order) if (k >> (depth - 1 - i)) & 1)
                for k in range(1 << depth)
            ]
        )
    return tables


def gram_kernel(
    plan, experts, count, teacher, student, gate, up, *rest
):
    if plan is None:
        acc, x, w, hid, masked, x_sem, w_sem = rest
    else:
        own, msg, x, w, hid, masked, acc, x_sem, w_sem = rest
    slots, both, _ = x.shape
    block = both // 2
    expert_total, _, two = w.shape
    width = two // 2
    live = count[0]

    def fresh(s):
        ok = s < live
        for t in range(s):
            ok = ok & (experts[t] != experts[s])
        return ok

    def x_copies(s):
        rows = pl.ds(s * block, block)
        return [
            pltpu.make_async_copy(student.at[rows], x.at[s, pl.ds(0, block)], x_sem.at[s, 0]),
            pltpu.make_async_copy(teacher.at[rows], x.at[s, pl.ds(block, block)], x_sem.at[s, 1]),
        ]

    def w_copies(e):
        return [
            pltpu.make_async_copy(gate.at[e], w.at[e, :, pl.ds(0, width)], w_sem.at[e, 0]),
            pltpu.make_async_copy(up.at[e], w.at[e, :, pl.ds(width, width)], w_sem.at[e, 1]),
        ]

    for s in range(slots):

        @pl.when(fresh(s))
        def _():
            for copy in w_copies(experts[s]):
                copy.start()

        @pl.when(s < live)
        def _():
            for copy in x_copies(s):
                copy.start()

    for s in range(slots):
        rows = pl.ds(s * block, block)

        @pl.when(fresh(s))
        def _():
            for copy in w_copies(experts[s]):
                copy.wait()

        @pl.when(s < live)
        def _():
            for copy in x_copies(s):
                copy.wait()
            expert = experts[s]
            out = jnp.dot(x[s], w[expert], preferred_element_type=jnp.float32)
            gate_out = out[:, :width]
            hidden = (gate_out / (1.0 + jnp.exp(-gate_out)) * out[:, width:]).astype(jnp.bfloat16)
            hid[rows, :width] = hidden[:block]
            hid[rows, width:] = hidden[block:]
            for e in range(expert_total):
                masked[e, rows] = jnp.where(expert == e, hidden[:block], jnp.zeros_like(hidden[:block]))

        @pl.when(s >= live)
        def _():
            hid[rows] = jnp.zeros((block, two), jnp.bfloat16)
            for e in range(expert_total):
                masked[e, rows] = jnp.zeros((block, width), jnp.bfloat16)

    for e in range(expert_total):
        gram = lax.dot_general(
            masked[e], hid[...], (((0,), (0,)), ((), ())), preferred_element_type=jnp.float32
        )
        if plan is None:
            acc[e * width : (e + 1) * width] = gram
        else:
            rows = acc.shape[1]
            per = width // rows
            acc[e * per : (e + 1) * per] = gram.reshape(per, rows, two)

    if plan is not None:
        me = lax.axis_index("dp")
        core = lax.rem(me, 2)
        chip = me // 2
        tables = block_offsets(plan)
        loads = []
        for k in range(len(tables[0])):
            mine = jnp.where(core == 0, tables[0][k], tables[1][k])
            theirs = jnp.where(core == 0, tables[1][k], tables[0][k])
            own[k] = acc[2 * (chip ^ mine) + core]
            there = 2 * (chip ^ theirs) + (1 - core)
            loads.append(lambda there=there: acc[there])
        write_codes(loads, msg)


def grams(teacher, student, experts, count, gate, up, ranks, plan):
    slots = experts.shape[0]
    block = teacher.shape[0] // slots
    depth = teacher.shape[1]
    expert_total, _, width = gate.shape
    two = 2 * width
    rows = expert_total * width // ranks
    scratch = [
        pltpu.VMEM((slots, 2 * block, depth), jnp.bfloat16),
        pltpu.VMEM((expert_total, depth, two), jnp.bfloat16),
        pltpu.VMEM((slots * block, two), jnp.bfloat16),
        pltpu.VMEM((expert_total, slots * block, width), jnp.bfloat16),
    ]
    sems = [pltpu.SemaphoreType.DMA((slots, 2)), pltpu.SemaphoreType.DMA((expert_total, 2))]
    if plan is None:
        out_shape = jax.ShapeDtypeStruct((expert_total * width, two), jnp.float32)
    else:
        scratch.append(pltpu.VMEM((ranks, rows, two), jnp.float32))
        out_shape = (
            jax.ShapeDtypeStruct((ranks // 2, rows, two), jnp.float32),
            message_shape(ranks // 2, rows, two),
        )
    smem = pl.BlockSpec(memory_space=pltpu.SMEM)
    hbm = pl.BlockSpec(memory_space=pl.ANY)
    return pl.pallas_call(
        functools.partial(gram_kernel, plan),
        out_shape=out_shape,
        in_specs=[smem, smem, hbm, hbm, hbm, hbm],
        scratch_shapes=scratch + sems,
        compiler_params=pltpu.CompilerParams(vmem_limit_bytes=51 << 20),
        name="grams",
    )(experts, count, teacher, student, gate, up)


def join_kernel(scaling, own, msg, *rest):
    count, rows, width = own.shape
    panels = width // LANES
    step = read_step(msg)
    if count == 1:
        (out,) = rest
        out[...] = (own[0] + read_block(msg, 0, rows, panels, step)) * scaling
        return
    keep, send, held = rest
    half = count // 2
    for k in range(half):
        held[k] = own[half + k] + read_block(msg, half + k, rows, panels, step)
    write_codes([lambda k=k: held[k] for k in range(half)], send)
    for k in range(half):
        keep[k] = own[k] + read_block(msg, k, rows, panels, step)


def join(own, msg, scaling):
    count, rows, width = own.shape
    if count == 1:
        out_shape = jax.ShapeDtypeStruct((rows, width), jnp.float32)
        scratch = []
    else:
        half = count // 2
        out_shape = (
            jax.ShapeDtypeStruct((half, rows, width), jnp.float32),
            message_shape(half, rows, width),
        )
        scratch = [pltpu.VMEM((half, rows, width), jnp.float32)]
    return pl.pallas_call(
        functools.partial(join_kernel, scaling),
        out_shape=out_shape,
        scratch_shapes=scratch,
        compiler_params=pltpu.CompilerParams(vmem_limit_bytes=32 << 20),
        name=f"join{count}",
    )(own, msg)


def local(teacher, student, experts, count, gate, up):
    ranks = lax.axis_size("dp")
    block = teacher.shape[0] // experts.shape[0]
    scaling = 1.0 / (block * ranks)
    total_rows = gate.shape[0] * gate.shape[2]
    rows = total_rows // ranks
    bits = ranks.bit_length() - 1
    coded = ranks >= 4 and ranks == 1 << bits and rows % 16 == 0 and gate.shape[2] % rows == 0
    if not coded:
        acc = grams(teacher, student, experts, count, gate, up, ranks, None)
        return lax.psum_scatter(acc, "dp", scatter_dimension=0, tiled=True) * scaling
    first = [1 << i for i in range(bits - 1)]
    second = first[1:2] + first[:1] + first[2:]
    own, msg = grams(teacher, student, experts, count, gate, up, ranks, (first, second))
    msg = lax.ppermute(msg, "dp", [(p, p ^ 1) for p in range(ranks)])
    for one, other in zip(first, second):
        own, msg = join(own, msg, scaling)
        msg = lax.ppermute(
            msg, "dp", [(p, p ^ (2 * (other if p % 2 else one))) for p in range(ranks)]
        )
    return join(own, msg, scaling)


def solution(mesh):
    return jax.shard_map(
        local,
        mesh=mesh,
        in_specs=(
            P(("groups", "dp"), None),
            P(("groups", "dp"), None),
            P(("groups", "dp")),
            P(("groups", "dp")),
            P("groups", None, None),
            P("groups", None, None),
        ),
        out_specs=P(("groups", "dp"), None),
        check_vma=False,
    )
```

time: 136 us -> 33.7 us (0.25)
  waiting for transfers between devices: 100 us -> 14.3 us
  between operations: 13.4 us -> 0.7 us
  starting transfers between devices: 0.01 us -> 10.1 us
  Pallas kernels: 0 us -> 7.83 us
  loops' own time: 7.61 us -> 0 us
  matrix products: 6.72 us -> 0 us
  local copies, waits for them, and re-layouts: 6.18 us -> 0.65 us
  other arithmetic: 1.58 us -> 0 us
    reduce_scatter x1 -> x0, waiting for transfers between devices: 100 us -> none  [local(): summed = lax.psum_scatter(accum, 'dp', scatter_dimension=0, tiled=True)]
    ppermute x0 -> x4, waiting for transfers between devices: none -> 14.3 us  [the longest x3 12.6 us: local(): lax.ppermute(msg, 'dp', [(p, p ^ 2 * (other if p % 2 else one)) for p in...]
    ppermute x0 -> x4, starting transfers between devices: none -> 10.1 us  [the longest x3 9.57 us: local(): lax.ppermute(msg, 'dp', [(p, p ^ 2 * (other if p % 2 else one)) for p in...]
    pallas_call x0 -> x5, Pallas kernels: none -> 7.83 us  [the longest x1 6.62 us: grams(): pl.pallas_call(functools.partial(gram_kernel, plan), out_shape=out_shape,...]
    another operation x1 -> x0, loops' own time: 7.61 us -> none  [accumulate_grams(): return lax.fori_loop(0, live_count, one_block, empty)]
    dot_general x6 -> x0, matrix products: 6.72 us -> none  [the longest x2 4.57 us: one_block(): gate_out = jnp.dot(stacked, gate_matrix, preferred_element_type=jnp.float32)]
    dynamic_slice x4 -> x0, local copies, waits for them, and re-layouts: 3.95 us -> none  [the longest x2 2.61 us: one_block(): lax.dynamic_slice_in_dim(teacher, slot_index * block_rows, block_rows, 0)]
    mul x1 -> x0, other arithmetic: 1.58 us -> none  [local(): return summed * scaling]
  transfers between devices with their start and end apart: 1 -> 4, of which waited for: 1 -> 4; matrix products, arithmetic and copies ran while one was open for 0% -> 0% of each run, Pallas kernels for 0% -> 0%
where the time goes in v1:
time: 33.7 us; the launch traced here: 33.5 us
  waiting for transfers between devices  14.3 us (42%)
  starting transfers between devices  10.1 us (30%)
  Pallas kernels  7.83 us (23%)
  between operations  0.7 us (2%)
  local copies, waits for them, and re-layouts  0.65 us (2%)
    ppermute x3, waiting for transfers between devices, local(): lax.ppermute(msg, 'dp', [(p, p ^ 2 * (other if p % 2 else one)) for p in...  12.6 us
    ppermute x3, starting transfers between devices, local(): lax.ppermute(msg, 'dp', [(p, p ^ 2 * (other if p % 2 else one)) for p in...  9.57 us
    pallas_call x1, Pallas kernels, grams(): pl.pallas_call(functools.partial(gram_kernel, plan), out_shape=out_shape,...  6.62 us
    ppermute x1, waiting for transfers between devices, local(): msg = lax.ppermute(msg, 'dp', [(p, p ^ 1) for p in range(ranks)])  1.64 us
    pallas_call x4, Pallas kernels, join(): pl.pallas_call(functools.partial(join_kernel, scaling), out_shape=out_sha...  1.21 us
  transfers between devices with their start and end apart: 4, of which 4 were waited for; matrix products, arithmetic and copies ran while one was open for 0% of the time, Pallas kernels for 0%

profile of v1, /device:TPU:0, one launch (start us, length us, event | category | flops | bytes accessed | tf_op | source)
XLA Modules:
  0.0 33.5 jit_solution(14510629760290835806)
XLA Ops:
  0.7 0.0 copy-start
  0.7 0.6 %copy-done = s32[6]{0:T(128)S(1)} copy-done((s32[6]{0:T(128)S(1)}, s32[6]{0:T(128)}, u32[]{:S(2)}) %copy-start) | copy-done | bytes 48
  1.3 6.6 %grams.1 = (f32[8,48,768]{2,1,0:T(8,128)S(1)}, s16[2320,128]{1,0:T(8,128)(2,1)S(1)}) custom-call(s32[6]{0:T(128)S(1)} %copy-done, s32[1]{0:T(128)S(6)} %copy.7.count, bf16[768,2048]{1,0:T(8,128)(2,1)} %teacher.1, bf16[768,2048]{1,0:T(8,128)(2,1)} %student.1, bf16[2,2048,384]{2,1,0:T(8,128)(2,1)} %gate.1, bf16[2,2048,384]{2,1,0:T(8,128)(2,1)} %up.1), custom_call_target="tpu_custom_call" | custom-call | tf_op jit(solution)/shard_map/grams/pallas_call | solution.py:193
  7.9 0.5 %collective-permute-start = (s16[2320,128]{1,0:T(8,128)(2,1)S(1)}, s16[2320,128]{1,0:T(8,128)(2,1)S(1)}, u32[]{:S(2)}, u32[]{:S(2)}) collective-permute-start(s16[2320,128]{1,0:T(8,128)(2,1)S(1)} %get-tuple-element.14), channel_id=1, source_target_pairs={{0,1},{1,0},{2,3},{3,2},{4,5},{5,4},{6,7},{7,6},{8,9},{9,8},{10,11... | collective-permute-start | bytes 1781768 | tf_op jit(solution)/shard_map/ppermute | solution.py:255
  8.4 1.6 %collective-permute-done.msg = s16[2320,128]{1,0:T(8,128)(2,1)S(1)} collective-permute-done((s16[2320,128]{1,0:T(8,128)(2,1)S(1)}, s16[2320,128]{1,0:T(8,128)(2,1)S(1)}, u32[]{:S(2)}, u32[]{:S(2)}) %collective-permute-start) | collective-permute-done | bytes 593952 | tf_op jit(solution)/shard_map/ppermute | solution.py:255
  10.1 0.3 join8.1
  10.4 6.8 %collective-permute-start.1 = (s16[1168,128]{1,0:T(8,128)(2,1)S(1)}, s16[1168,128]{1,0:T(8,128)(2,1)S(1)}, u32[]{:S(2)}, u32[]{:S(2)}) collective-permute-start(s16[1168,128]{1,0:T(8,128)(2,1)S(1)} %get-tuple-element.16), channel_id=1, source_target_pairs={{0,2},{1,5},{2,0},{3,7},{4,6},{5,1},{6,4},{7,3},{8,10},{9,13},{10,... | collective-permute-start | bytes 897032 | tf_op jit(solution)/shard_map/ppermute | solution.py:258
  17.2 4.7 %collective-permute-done.1.msg = s16[1168,128]{1,0:T(8,128)(2,1)S(1)} collective-permute-done((s16[1168,128]{1,0:T(8,128)(2,1)S(1)}, s16[1168,128]{1,0:T(8,128)(2,1)S(1)}, u32[]{:S(2)}, u32[]{:S(2)}) %collective-permute-start.1) | collective-permute-done | bytes 299040 | tf_op jit(solution)/shard_map/ppermute | solution.py:258
  22.0 0.1 join4.1
  22.1 0.1 collective-permute-start.2
  22.2 5.2 %collective-permute-done.2.msg = s16[592,128]{1,0:T(8,128)(2,1)S(1)} collective-permute-done((s16[592,128]{1,0:T(8,128)(2,1)S(1)}, s16[592,128]{1,0:T(8,128)(2,1)S(1)}, u32[]{:S(2)}, u32[]{:S(2)}) %collective-permute-start.2) | collective-permute-done | bytes 151584 | tf_op jit(solution)/shard_map/ppermute | solution.py:258
  27.4 0.1 join2.1
  27.5 2.7 %collective-permute-start.3 = (s16[304,128]{1,0:T(8,128)(2,1)S(1)}, s16[304,128]{1,0:T(8,128)(2,1)S(1)}, u32[]{:S(2)}, u32[]{:S(2)}) collective-permute-start(s16[304,128]{1,0:T(8,128)(2,1)S(1)} %get-tuple-element.20), channel_id=1, source_target_pairs={{0,8},{1,9},{2,10},{3,11},{4,12},{5,13},{6,14},{7,15},{8,0},{9,1},... | collective-permute-start | bytes 233480 | tf_op jit(solution)/shard_map/ppermute | solution.py:258
  30.1 2.7 %collective-permute-done.3.msg = s16[304,128]{1,0:T(8,128)(2,1)S(1)} collective-permute-done((s16[304,128]{1,0:T(8,128)(2,1)S(1)}, s16[304,128]{1,0:T(8,128)(2,1)S(1)}, u32[]{:S(2)}, u32[]{:S(2)}) %collective-permute-start.3) | collective-permute-done | bytes 77856 | tf_op jit(solution)/shard_map/ppermute | solution.py:258
  32.8 0.7 %join1.1 = f32[48,768]{1,0:T(8,128)} custom-call(f32[1,48,768]{2,1,0:T(8,128)S(1)} %get-tuple-element.19.own, s16[304,128]{1,0:T(8,128)(2,1)S(1)} %collective-permute-done.3.msg), custom_call_target="tpu_custom_call" | custom-call | tf_op jit(solution)/shard_map/join1/pallas_call | solution.py:232
Async XLA Ops:
  0.7 0.7 %copy-start = (s32[6]{0:T(128)S(1)}, s32[6]{0:T(128)}, u32[]{:S(2)}) copy-start(s32[6]{0:T(128)} %experts.1) | copy-start | bytes 76
  7.9 2.1 %collective-permute-start = (s16[2320,128]{1,0:T(8,128)(2,1)S(1)}, s16[2320,128]{1,0:T(8,128)(2,1)S(1)}, u32[]{:S(2)}, u32[]{:S(2)}) collective-permute-start(s16[2320,128]{1,0:T(8,128)(2,1)S(1)} %get-tuple-element.14), channel_id=1, source_target_pairs={{0,1},{1,0},{2,3},{3,2},{4,5},{5,4},{6,7},{7,6},{8,9},{9,8},{10,11... | collective-permute-start | bytes 1781768 | tf_op jit(solution)/shard_map/ppermute | solution.py:255
  10.4 11.6 %collective-permute-start.1 = (s16[1168,128]{1,0:T(8,128)(2,1)S(1)}, s16[1168,128]{1,0:T(8,128)(2,1)S(1)}, u32[]{:S(2)}, u32[]{:S(2)}) collective-permute-start(s16[1168,128]{1,0:T(8,128)(2,1)S(1)} %get-tuple-element.16), channel_id=1, source_target_pairs={{0,2},{1,5},{2,0},{3,7},{4,6},{5,1},{6,4},{7,3},{8,10},{9,13},{10,... | collective-permute-start | bytes 897032 | tf_op jit(solution)/shard_map/ppermute | solution.py:258
  22.1 5.3 %collective-permute-start.2 = (s16[592,128]{1,0:T(8,128)(2,1)S(1)}, s16[592,128]{1,0:T(8,128)(2,1)S(1)}, u32[]{:S(2)}, u32[]{:S(2)}) collective-permute-start(s16[592,128]{1,0:T(8,128)(2,1)S(1)} %get-tuple-element.18), channel_id=1, source_target_pairs={{0,4},{1,3},{2,6},{3,1},{4,0},{5,7},{6,2},{7,5},{8,12},{9,11},{10,... | collective-permute-start | bytes 454664 | tf_op jit(solution)/shard_map/ppermute | solution.py:258
  27.5 5.4 %collective-permute-start.3 = (s16[304,128]{1,0:T(8,128)(2,1)S(1)}, s16[304,128]{1,0:T(8,128)(2,1)S(1)}, u32[]{:S(2)}, u32[]{:S(2)}) collective-permute-start(s16[304,128]{1,0:T(8,128)(2,1)S(1)} %get-tuple-element.20), channel_id=1, source_target_pairs={{0,8},{1,9},{2,10},{3,11},{4,12},{5,13},{6,14},{7,15},{8,0},{9,1},... | collective-permute-start | bytes 233480 | tf_op jit(solution)/shard_map/ppermute | solution.py:258
